TPU v7x, 256 devices: a whole 4x4x8 slice. The times are simulated.
256 devices in a mesh: pair: 32 (over y, z), tm: 8 (over x, core).
Axes of the slice: x: 4, y: 4, z: 8, core: 2. Of those that a mesh axis runs over, the one named last changes fastest.
Arguments:
- spectra: bfloat16 [4096, 16, 2, 4096], P('pair', 'tm'), may hold values from -6 to 6
- send_rows: int32 [32, 32, 4], P('pair'), may hold values from 0 to 127
- pair_list: int32 [2, 12288], P(None, 'pair'), may hold values from 0 to 127
- pair_count: int32 [32], P('pair'), may hold values from 128 to 384, as said below
Outputs:
- correlations: float32 [12288, 1024], P(('pair', 'tm'))
Inputs may be any that keep to these rules, and one draw needn't show every extreme that they name: `pair_list`: indices into one owner's 32 * 4 received rows. `pair_count`: some owner has all 384 slots live; slots at and after the count are empty.
All inputs are finite; a program needn't handle non-finite values.
Results may differ from a plain program's by a relative error of at most 0.0003.
Values may be sent and summed in bfloat16 or wider, within the bound.
A program may use at most 192 MiB of HBM per device.

v0:
```python
import math

import jax
import jax.numpy as jnp
from jax import lax
from jax.sharding import PartitionSpec as P

LAGS = 1024


def phase_tables(begin, block, bins, lags):
    freq = jnp.arange(block, dtype=jnp.int32) + begin
    delay = jnp.arange(lags, dtype=jnp.int32) - lags // 2
    turns = freq[:, None] * delay[None, :] % (2 * bins)
    angle = turns.astype(jnp.float32) * (math.pi / bins)
    return (jnp.cos(angle), jnp.sin(angle))


def transform(stacked, scale):
    bins = stacked.shape[2]
    block = min(512, bins)
    total = jnp.zeros((stacked.shape[0], LAGS), jnp.float32)
    for begin in range(0, bins, block):
        cosine, sine = phase_tables(begin, block, bins, LAGS)
        real_part = stacked[:, 0, begin : begin + block]
        imag_part = stacked[:, 1, begin : begin + block]
        total = total + jnp.dot(real_part, cosine, precision=lax.Precision.HIGHEST)
        total = total - jnp.dot(imag_part, sine, precision=lax.Precision.HIGHEST)
    return total * scale


def shards(spectra, send_rows, pair_list, pair_count):
    owners = lax.axis_size("pair")
    capacity = send_rows.shape[2]
    windows_here = spectra.shape[1]
    bins = spectra.shape[3]
    pairs_here = pair_list.shape[1]
    outgoing = jnp.take(spectra, send_rows.reshape(-1), axis=0)
    outgoing = outgoing.reshape(owners, capacity, windows_here, 2, bins)
    left_ids = pair_list[0]
    right_ids = pair_list[1]
    active = (jnp.arange(pairs_here, dtype=jnp.int32) < pair_count[0]).astype(jnp.float32)[
        :, None, None
    ]
    arrived = lax.all_to_all(outgoing, "pair", split_axis=0, concat_axis=0, tiled=True)
    width = arrived.shape[4]
    arrived_rows = arrived.reshape(owners * capacity, windows_here, 2, width)
    stacked = jnp.zeros((pairs_here, 2, width), jnp.float32)
    for window in range(windows_here):
        left_rows = jnp.take(arrived_rows[:, window], left_ids, axis=0).astype(jnp.float32)
        right_rows = jnp.take(arrived_rows[:, window], right_ids, axis=0).astype(jnp.float32)
        real_part = left_rows[:, 0] * right_rows[:, 0] + left_rows[:, 1] * right_rows[:, 1]
        imag_part = left_rows[:, 1] * right_rows[:, 0] - left_rows[:, 0] * right_rows[:, 1]
        stacked = stacked + jnp.stack([real_part, imag_part], axis=1)
    stacked = stacked * active
    scale = (2.0 * bins * windows_here * lax.axis_size("tm")) ** (-0.5)
    share = lax.psum_scatter(stacked, "tm", scatter_dimension=0, tiled=True)
    return transform(share, scale)


def solution(mesh):
    in_specs = (P("pair", "tm", None, None), P("pair", None, None), P(None, "pair"), P("pair"))
    out_specs = P(("pair", "tm"), None)
    return jax.shard_map(shards, mesh=mesh, in_specs=in_specs, out_specs=out_specs, check_vma=False)
```

profile of v0, /device:TPU:1, one launch (start us, length us, event | category | flops | bytes accessed | tf_op | source)
XLA Modules:
  0.0 666.0 jit_solution(8676491762072556387)
XLA Ops:
  6.5 0.8 copy.10
  7.3 0.7 compare_and_fusion.2
  8.0 0.1 reshape.89
  8.1 0.1 copy.9
  8.2 14.0 %gather_fusion = bf16[128,2,2,4096]{3,2,1,0:T(2,128)(2,1)} fusion(bf16[128,2,2,4096]{3,2,1,0:T(2,128)(2,1)} %param.6, s32[1024]{0:T(1024)S(1)} %pad_clamp_fusion.2), kind=kCustom, calls=%fused_computation.4 | custom fusion | bytes 8389120 | tf_op jit(solution)/shard_map/jit(_take)/gather | solution.py:38
  22.3 8.0 %broadcast_select_fusion.4 = bf16[32,4,2,2,4096]{4,3,2,1,0:T(2,128)(2,1)} fusion(bf16[32,4,2,2,4096]{4,3,2,1,0:T(2,128)(2,1)} %bitcast.63, pred[32,4]{1,0:T(8,128)(4,1)S(1)} %copy.9), kind=kLoop, calls=%fused_computation.11 | loop fusion | flops 2097152 | bytes 8388736 | tf_op jit(solution)/shard_map/jit(_take)/select_n | solution.py:38
  30.2 0.0 copy-start.2
  30.2 12.3 %all-to-all-start = ((bf16[32,4,2,2,4096]{4,3,2,1,0:T(2,128)(2,1)}), bf16[32,4,2,2,4096]{4,3,2,1,0:T(2,128)(2,1)}, u32[]{:S(2)}, u32[]{:S(2)}) async-start(bf16[32,4,2,2,4096]{4,3,2,1,0:T(2,128)(2,1)} %broadcast_select_fusion.4), calls=%async_computation | async-start | bytes 8388608 | tf_op jit(solution)/shard_map/all_to_all | solution.py:45
  42.5 0.6 all-reduce.3.cloned.1.call-start
  43.8 0.0 copy-done.2
  43.9 91.4 %all-to-all-done = bf16[32,4,2,2,4096]{4,3,2,1,0:T(2,128)(2,1)} async-done(((bf16[32,4,2,2,4096]{4,3,2,1,0:T(2,128)(2,1)}), bf16[32,4,2,2,4096]{4,3,2,1,0:T(2,128)(2,1)}, u32[]{:S(2)}, u32[]{:S(2)}) %all-to-all-start) | async-done | bytes 4194336 | tf_op jit(solution)/shard_map/all_to_all | solution.py:45
  135.3 7.1 %slice_bitcast_fusion = (bf16[128,2,4096]{2,1,0:T(2,128)(2,1)S(1)}, bf16[128,2,4096]{2,1,0:T(2,128)(2,1)}) fusion(bf16[128,2,2,4096]{3,2,1,0:T(2,128)(2,1)} %bitcast.3), kind=kLoop, calls=%fused_computation.82 | loop fusion | bytes 8388608 | tf_op jit(solution)/shard_map/squeeze | solution.py:50
  142.4 21.8 %gather_fusion.1 = bf16[384,2,4096]{2,1,0:T(2,128)(2,1)} fusion(bf16[128,2,4096]{2,1,0:T(2,128)(2,1)} %get-tuple-element.29, s32[1024]{0:T(1024)S(1)} %pad_clamp_fusion.1), kind=kCustom, calls=%fused_computation.clone | custom fusion | bytes 12584448 | tf_op jit(solution)/shard_map/jit(_take)/gather | solution.py:50
  164.2 20.2 %gather_fusion.3 = bf16[384,2,4096]{2,1,0:T(2,128)(2,1)} fusion(bf16[128,2,4096]{2,1,0:T(2,128)(2,1)S(1)} %get-tuple-element.28, s32[1024]{0:T(1024)S(1)} %pad_clamp_fusion.1), kind=kCustom, calls=%fused_computation.2.clone | custom fusion | bytes 12584448 | tf_op jit(solution)/shard_map/jit(_take)/gather | solution.py:50
  184.4 21.8 %gather_fusion.2 = bf16[384,2,4096]{2,1,0:T(2,128)(2,1)} fusion(bf16[128,2,4096]{2,1,0:T(2,128)(2,1)} %get-tuple-element.29, s32[1024]{0:T(1024)S(1)} %pad_clamp_fusion), kind=kCustom, calls=%fused_computation.1.clone | custom fusion | bytes 12584448 | tf_op jit(solution)/shard_map/jit(_take)/gather | solution.py:51
  206.2 20.3 %gather_fusion.4 = bf16[384,2,4096]{2,1,0:T(2,128)(2,1)} fusion(bf16[128,2,4096]{2,1,0:T(2,128)(2,1)S(1)} %get-tuple-element.28, s32[1024]{0:T(1024)S(1)} %pad_clamp_fusion), kind=kCustom, calls=%fused_computation.3.clone | custom fusion | bytes 12584448 | tf_op jit(solution)/shard_map/jit(_take)/gather | solution.py:51
  226.5 0.0 copy-start
  226.5 0.0 copy-start.1
  226.5 17.6 %fusion.2 = (f32[384,2,4096]{2,1,0:T(2,128)}, f32[384,2,4096]{2,1,0:T(2,128)}) fusion(bf16[384,2,4096]{2,1,0:T(2,128)(2,1)} %gather_fusion.3, pred[384]{0:T(512)(128)(4,1)S(1)} %get-tuple-element.37, bf16[384,2,4096]{2,1,0:T(2,128)(2,1)} %gather_fusion.1), kind=kLoop, calls=%fused_computation.13 | loop fusion | flops 12582912 | bytes 37749120 | tf_op jit(solution)/shard_map/convert_element_type | solution.py:50
  244.1 0.0 copy-done
  244.1 0.0 copy-done.1
  244.1 13.6 %fusion.4 = (f32[384,2,4096]{2,1,0:T(2,128)}, f32[384,2,4096]{2,1,0:T(2,128)}) fusion(bf16[384,2,4096]{2,1,0:T(2,128)(2,1)S(1)} %copy-done.1, pred[384]{0:T(512)(128)(4,1)S(1)} %get-tuple-element.36, bf16[384,2,4096]{2,1,0:T(2,128)(2,1)S(1)} %copy-done), kind=kLoop, calls=%fused_computation.15 | loop fusion | flops 12582912 | bytes 37749120 | tf_op jit(solution)/shard_map/convert_element_type | solution.py:51
  257.7 34.5 %multiply_add_fusion = (f32[384,1,4096]{2,1,0:T(1,128)}, f32[384,1,4096]{2,1,0:T(1,128)}) fusion(f32[384,2,4096]{2,1,0:T(2,128)} %get-tuple-element.32, f32[384,2,4096]{2,1,0:T(2,128)} %get-tuple-element.30), kind=kLoop, calls=%fused_computation.17 | loop fusion | flops 9437184 | bytes 37748736 | tf_op jit(solution)/shard_map/add | solution.py:52
  292.3 33.9 %multiply_add_fusion.1 = (f32[384,1,4096]{2,1,0:T(1,128)}, f32[384,1,4096]{2,1,0:T(1,128)}) fusion(f32[384,2,4096]{2,1,0:T(2,128)} %get-tuple-element.33, f32[384,2,4096]{2,1,0:T(2,128)} %get-tuple-element.31), kind=kLoop, calls=%fused_computation.19 | loop fusion | flops 9437184 | bytes 37748736 | tf_op jit(solution)/shard_map/add | solution.py:52
  326.2 28.9 %fusion = f32[384,2,4096]{2,1,0:T(2,128)} fusion(f32[384,1,4096]{2,1,0:T(1,128)} %get-tuple-element.11, f32[384,1,4096]{2,1,0:T(1,128)} %get-tuple-element.10, f32[384,1,4096]{2,1,0:T(1,128)} %get-tuple-element.9, f32[384,1,4096]{2,1,0:T(1,128)} %get-tuple-element.8, f32[384]{0:T(512)S(1)} %fusion.160), kind=kLoop, calls=%fused_computation.6 | loop fusion | flops 12582912 | bytes 37750272 | tf_op jit(solution)/shard_map/mul | solution.py:55
  355.1 0.0 copy-start.3
  355.1 0.0 all-reduce.3.cloned.1.call-update
  355.1 0.6 copy-done.3
  355.7 0.6 dynamic-slice
  357.1 147.8 %all-reduce.3.cloned.1.call-done = f32[384,2,4096]{2,1,0:T(2,128)} async-done(((f32[384,2,4096]{2,1,0:T(2,128)}), f32[384,2,4096]{2,1,0:T(2,128)}) %all-reduce.3.cloned.1.call-update) | async-done | bytes 12582928
  504.9 5.2 fusion.226
  510.1 9.5 %fusion.53 = f32[48,1024]{1,0:T(8,128)S(1)} fusion(s32[512]{0:T(512)S(1)} %iota_add_fusion.7, s32[1024]{0:T(1024)S(1)} %iota_add_fusion, f32[48,1,512]{2,1,0:T(1,128)S(1)} %get-tuple-element.23), kind=kOutput, calls=%fused_computation.108 | convolution fusion | flops 309329920 | bytes 301056 | tf_op jit(solution)/shard_map/dot_general | solution.py:28
  519.5 9.0 %fusion.55 = f32[48,1024]{1,0:T(8,128)S(1)} fusion(s32[512]{0:T(512)S(1)} %iota_add_fusion.7, s32[1024]{0:T(1024)S(1)} %iota_add_fusion, f32[48,1,512]{2,1,0:T(1,128)S(1)} %get-tuple-element.24), kind=kOutput, calls=%fused_computation.110 | convolution fusion | flops 309329920 | bytes 301056 | tf_op jit(solution)/shard_map/dot_general | solution.py:27
  528.5 9.6 %fusion.57 = f32[48,1024]{1,0:T(8,128)S(1)} fusion(s32[1024]{0:T(1024)S(1)} %iota_add_fusion, f32[48,1,512]{2,1,0:T(1,128)S(1)} %get-tuple-element.25), kind=kOutput, calls=%fused_computation.112 | convolution fusion | flops 309329920 | bytes 299008 | tf_op jit(solution)/shard_map/dot_general | solution.py:28
  538.1 9.1 %fusion.45 = f32[48,1024]{1,0:T(8,128)S(1)} fusion(s32[512]{0:T(512)S(1)} %iota_add_fusion.5, s32[1024]{0:T(1024)S(1)} %iota_add_fusion, f32[48,1,512]{2,1,0:T(1,128)S(1)} %get-tuple-element.19), kind=kOutput, calls=%fused_computation.100 | convolution fusion | flops 309329920 | bytes 301056 | tf_op jit(solution)/shard_map/dot_general | solution.py:28
  547.2 9.2 %fusion.47 = f32[48,1024]{1,0:T(8,128)S(1)} fusion(s32[512]{0:T(512)S(1)} %iota_add_fusion.5, s32[1024]{0:T(1024)S(1)} %iota_add_fusion, f32[48,1,512]{2,1,0:T(1,128)S(1)} %get-tuple-element.20), kind=kOutput, calls=%fused_computation.102 | convolution fusion | flops 309329920 | bytes 301056 | tf_op jit(solution)/shard_map/dot_general | solution.py:27
  556.3 9.5 %fusion.37 = f32[48,1024]{1,0:T(8,128)S(1)} fusion(s32[512]{0:T(512)S(1)} %iota_add_fusion.3, s32[1024]{0:T(1024)S(1)} %iota_add_fusion, f32[48,1,512]{2,1,0:T(1,128)S(1)} %get-tuple-element.15), kind=kOutput, calls=%fused_computation.92 | convolution fusion | flops 309329920 | bytes 301056 | tf_op jit(solution)/shard_map/dot_general | solution.py:28
  565.8 9.1 %fusion.39 = f32[48,1024]{1,0:T(8,128)S(1)} fusion(s32[512]{0:T(512)S(1)} %iota_add_fusion.3, s32[1024]{0:T(1024)S(1)} %iota_add_fusion, f32[48,1,512]{2,1,0:T(1,128)S(1)} %get-tuple-element.16), kind=kOutput, calls=%fused_computation.94 | convolution fusion | flops 309329920 | bytes 301056 | tf_op jit(solution)/shard_map/dot_general | solution.py:27
  575.0 9.0 %fusion.31 = f32[48,1024]{1,0:T(8,128)S(1)} fusion(s32[512]{0:T(512)S(1)} %iota_add_fusion.1, s32[1024]{0:T(1024)S(1)} %iota_add_fusion, f32[48,1,512]{2,1,0:T(1,128)S(1)} %get-tuple-element.13), kind=kOutput, calls=%fused_computation.86 | convolution fusion | flops 309329920 | bytes 301056 | tf_op jit(solution)/shard_map/dot_general | solution.py:27
  584.0 9.3 %fusion.29 = f32[48,1024]{1,0:T(8,128)S(1)} fusion(s32[512]{0:T(512)S(1)} %iota_add_fusion.1, s32[1024]{0:T(1024)S(1)} %iota_add_fusion, f32[48,1,512]{2,1,0:T(1,128)S(1)} %get-tuple-element.27), kind=kOutput, calls=%fused_computation.84 | convolution fusion | flops 309329920 | bytes 301056 | tf_op jit(solution)/shard_map/dot_general | solution.py:28
  593.2 9.4 %fusion.51 = f32[48,1024]{1,0:T(8,128)S(1)} fusion(s32[512]{0:T(512)S(1)} %iota_add_fusion.6, s32[1024]{0:T(1024)S(1)} %iota_add_fusion, f32[48,1,512]{2,1,0:T(1,128)S(1)} %get-tuple-element.22), kind=kOutput, calls=%fused_computation.106 | convolution fusion | flops 309329920 | bytes 301056 | tf_op jit(solution)/shard_map/dot_general | solution.py:27
  602.7 9.1 %fusion.43 = f32[48,1024]{1,0:T(8,128)S(1)} fusion(s32[512]{0:T(512)S(1)} %iota_add_fusion.4, s32[1024]{0:T(1024)S(1)} %iota_add_fusion, f32[48,1,512]{2,1,0:T(1,128)S(1)} %get-tuple-element.18), kind=kOutput, calls=%fused_computation.98 | convolution fusion | flops 309329920 | bytes 301056 | tf_op jit(solution)/shard_map/dot_general | solution.py:27
  611.8 9.0 %fusion.35 = f32[48,1024]{1,0:T(8,128)S(1)} fusion(s32[512]{0:T(512)S(1)} %iota_add_fusion.2, s32[1024]{0:T(1024)S(1)} %iota_add_fusion, f32[48,1,512]{2,1,0:T(1,128)S(1)} %get-tuple-element.14), kind=kOutput, calls=%fused_computation.90 | convolution fusion | flops 309329920 | bytes 301056 | tf_op jit(solution)/shard_map/dot_general | solution.py:27
  620.8 9.8 %fusion.73 = f32[48,1024]{1,0:T(8,128)S(1)} fusion(f32[48,1024]{1,0:T(8,128)S(1)} %fusion.51, f32[48,1024]{1,0:T(8,128)S(1)} %fusion.53, f32[48,1024]{1,0:T(8,128)S(1)} %fusion.55, f32[48,1024]{1,0:T(8,128)S(1)} %fusion.57, s32[1024]{0:T(1024)S(1)} %iota_add_fusion, f32[48,1,512]{2,1,0:T(1,128)S(1)} %get-tuple-element.26), kind=kOutput, calls=%fused_computation.122 | convolution fusion | flops 309526528 | bytes 1085440 | tf_op jit(solution)/shard_map/dot_general | solution.py:27
  630.6 9.1 %fusion.85 = f32[48,1024]{1,0:T(8,128)S(1)} fusion(f32[48,1024]{1,0:T(8,128)S(1)} %fusion.43, f32[48,1024]{1,0:T(8,128)S(1)} %fusion.45, f32[48,1024]{1,0:T(8,128)S(1)} %fusion.47, f32[48,1024]{1,0:T(8,128)S(1)} %fusion.73, s32[512]{0:T(512)S(1)} %iota_add_fusion.6, s32[1024]{0:T(1024)S(1)} %iota_add_fusion, f32[48,1,512]{2,1,0:T(1,128)S(1)} %get-tuple-element.21), kind=kOutput, calls=%fused_computation.126 | convolution fusion | flops 309526528 | bytes 1087488 | tf_op jit(solution)/shard_map/dot_general | solution.py:28
  639.7 9.2 %fusion.97 = f32[48,1024]{1,0:T(8,128)S(1)} fusion(f32[48,1024]{1,0:T(8,128)S(1)} %fusion.35, f32[48,1024]{1,0:T(8,128)S(1)} %fusion.37, f32[48,1024]{1,0:T(8,128)S(1)} %fusion.39, f32[48,1024]{1,0:T(8,128)S(1)} %fusion.85, s32[512]{0:T(512)S(1)} %iota_add_fusion.4, s32[1024]{0:T(1024)S(1)} %iota_add_fusion, f32[48,1,512]{2,1,0:T(1,128)S(1)} %get-tuple-element.17), kind=kOutput, calls=%fused_computation.130 | convolution fusion | flops 309526528 | bytes 1087488 | tf_op jit(solution)/shard_map/dot_general | solution.py:28
  648.9 10.0 %fusion.109 = f32[48,1024]{1,0:T(8,128)} fusion(f32[48,1024]{1,0:T(8,128)S(1)} %fusion.29, f32[48,1024]{1,0:T(8,128)S(1)} %fusion.31, f32[48,1024]{1,0:T(8,128)S(1)} %fusion.97, s32[512]{0:T(512)S(1)} %iota_add_fusion.2, s32[1024]{0:T(1024)S(1)} %iota_add_fusion, f32[48,1,512]{2,1,0:T(1,128)S(1)} %get-tuple-element.12), kind=kOutput, calls=%fused_computation.134 | convolution fusion | flops 309526528 | bytes 890880 | tf_op jit(solution)/shard_map/dot_general | solution.py:28
  (16 shorter events, 0.1 us)
Async XLA Ops:
  30.2 13.5 %copy-start.2 = (s32[2,384]{1,0:T(2,128)S(1)}, s32[2,384]{1,0:T(2,128)}, u32[]{:S(2)}) copy-start(s32[2,384]{1,0:T(2,128)} %param.8) | copy-start | bytes 9220
  30.2 105.1 %all-to-all-start = ((bf16[32,4,2,2,4096]{4,3,2,1,0:T(2,128)(2,1)}), bf16[32,4,2,2,4096]{4,3,2,1,0:T(2,128)(2,1)}, u32[]{:S(2)}, u32[]{:S(2)}) async-start(bf16[32,4,2,2,4096]{4,3,2,1,0:T(2,128)(2,1)} %broadcast_select_fusion.4), calls=%async_computation | async-start | bytes 8388608 | tf_op jit(solution)/shard_map/all_to_all | solution.py:45
  42.5 462.3 %all-reduce.3.cloned.1.call-start = ((), (), s32[]{:S(2)}) async-start(), calls=%async_computation.1 | async-start | bytes 25165824
  226.5 17.6 %copy-start = (bf16[384,2,4096]{2,1,0:T(2,128)(2,1)S(1)}, bf16[384,2,4096]{2,1,0:T(2,128)(2,1)}, u32[]{:S(2)}) copy-start(bf16[384,2,4096]{2,1,0:T(2,128)(2,1)} %gather_fusion.2) | copy-start | bytes 18874372
  226.5 17.6 %copy-start.1 = (bf16[384,2,4096]{2,1,0:T(2,128)(2,1)S(1)}, bf16[384,2,4096]{2,1,0:T(2,128)(2,1)}, u32[]{:S(2)}) copy-start(bf16[384,2,4096]{2,1,0:T(2,128)(2,1)} %gather_fusion.4) | copy-start | bytes 18874372
  355.1 0.7 copy-start.3
Sparse Core Ops, SparseCore 0:
  355.2 149.6 all-reduce.2
where the time goes:
time: 672 us; the launch traced here: 666 us
  waiting for transfers between devices  239 us (36%)
  matrix products  149 us (22%)
  other arithmetic  137 us (20%)
  local copies, waits for them, and re-layouts  113 us (17%)
  between operations  15.2 us (2%)
  starting transfers between devices  12.9 us (2%)
    unnamed x2, waiting for transfers between devices  148 us
    all_to_all x1, waiting for transfers between devices, shards(): lax.all_to_all(outgoing, 'pair', split_axis=0, concat_axis=0, tiled=True)  91.4 us
    dot_general x8, matrix products, transform(): total = total - jnp.dot(imag_part, sine, precision=lax.Precision.HIGHEST)  75.1 us
    dot_general x8, matrix products, transform(): total = total + jnp.dot(real_part, cosine, precision=lax.Precision.HIGHEST)  73.6 us
    add x2, other arithmetic, shards(): left_rows[:, 0] * right_rows[:, 0] + left_rows[:, 1] * right_rows[:, 1]  68.5 us
    gather x2, local copies, waits for them, and re-layouts, shards(): jnp.take(arrived_rows[:, window], right_ids, axis=0).astype(jnp.float32)  42.1 us
    gather x2, local copies, waits for them, and re-layouts, shards(): jnp.take(arrived_rows[:, window], left_ids, axis=0).astype(jnp.float32)  42 us
    mul x1, other arithmetic, shards(): stacked = stacked * active  28.9 us
  transfers between devices with their start and end apart: 2, of which 2 were waited for; matrix products, arithmetic and copies ran while one was open for 0% of the time, Pallas kernels for 0%

commit v1 on v0

v1 whole, which is shorter than its diff:
```python
import functools
import math

import jax
import jax.numpy as jnp
import ml_dtypes
import numpy as np
from jax import lax
from jax.experimental import pallas as pl
from jax.experimental.pallas import tpu as pltpu
from jax.sharding import PartitionSpec as P

MESH = pl.DeviceIdType.MESH
LAGS = 1024
LANES = 128
GROUP = 8
F32 = jnp.float32
BF16 = jnp.bfloat16


def lag_table(bins, lags):
    freq = np.arange(bins, dtype=np.int64)
    delay = np.arange(lags, dtype=np.int64) - lags // 2
    angle = (freq[:, None] * delay[None, :] % (2 * bins)).astype(np.float64) * (math.pi / bins)
    both = np.stack([np.cos(angle), -np.sin(angle)]).astype(np.float32)
    both = both.reshape(2, bins // LANES, LANES, lags).transpose(1, 0, 2, 3).reshape(bins // LANES, 2 * LANES, lags)
    high = both.astype(ml_dtypes.bfloat16)
    low = (both - high.astype(np.float32)).astype(ml_dtypes.bfloat16)
    return np.stack([high, low], axis=1)


def kernel(dims, x_hbm, rows_ref, pairs_ref, count_ref, table_hbm, out_ref,
           *scratch):
    owners, times, capacity, windows, groups, npairs, chunks, scale = dims
    xbufs, scratch = scratch[:groups], scratch[groups:]
    stage, sendbuf, recvbuf, ohot, dhi, dlo, tbuf, acc, summed, xsem, tsem, ssem, rsem, lsem, psem, qsem = scratch
    me = lax.axis_index("pair")
    tm = lax.axis_index("tm")
    share = npairs // times

    def load_x(g, w):
        rows = pl.ds((w * groups + g) * 2 * GROUP, 2 * GROUP)
        to = pl.ds(w * 2 * GROUP, 2 * GROUP)
        return pltpu.make_async_copy(x_hbm.at[:, rows, :], xbufs[g].at[:, to, :], xsem.at[g, w])

    def load_table(g):
        return pltpu.make_async_copy(table_hbm.at[pl.ds(g * GROUP, GROUP)], tbuf.at[g % 2], tsem.at[g])

    for w in range(windows):
        load_x(0, w).start()

    barrier = pltpu.get_barrier_semaphore()

    def greet_owner(i, _):
        pl.semaphore_signal(barrier, inc=1, device_id=(lax.rem(me + i, owners), tm), device_id_type=MESH)
        return 0

    def greet_time(i, _):
        pl.semaphore_signal(barrier, inc=1, device_id=(me, lax.rem(tm + i, times)), device_id_type=MESH)
        return 0

    lax.fori_loop(1, owners, greet_owner, 0)
    lax.fori_loop(1, times, greet_time, 0)
    for g in range(1, groups):
        for w in range(windows):
            load_x(g, w).start()
    load_table(0).start()
    load_table(1).start()

    def prepare(g):
        for w in range(windows):
            load_x(g, w).wait()

        def one(o, _):
            base = lax.rem(o, 4) * (16 * GROUP)
            for k in range(capacity):
                r = rows_ref[k, o]
                for w in range(windows):
                    v = xbufs[g][r, w * 2 * GROUP : (w + 1) * 2 * GROUP, :]
                    stage[pl.ds(base + k * windows + w, 2 * GROUP, stride=8), :] = v.astype(F32)
            for t in range(GROUP):
                sendbuf[g, o, :, t * LANES : (t + 1) * LANES] = stage[pl.ds(base + t * 16, 16), :].astype(BF16)
            return 0

        lax.fori_loop(0, owners, one, 0, unroll=2)

    def lanes(c):
        g, t0, nt = chunks[c]
        return pl.ds(t0 * LANES, nt * LANES)

    def send(c):
        g = chunks[c][0]

        def one(i, _):
            to = lax.rem(me + i, owners)
            pltpu.make_async_remote_copy(
                src_ref=sendbuf.at[g, to, :, lanes(c)], dst_ref=recvbuf.at[g, me, :, lanes(c)],
                send_sem=ssem.at[c], recv_sem=rsem.at[c], device_id=(to, tm), device_id_type=MESH,
            ).start()
            return 0

        lax.fori_loop(1, owners, one, 0)
        pltpu.make_async_copy(sendbuf.at[g, me, :, lanes(c)], recvbuf.at[g, me, :, lanes(c)], lsem.at[c]).start()

    def wait_received(c):
        g = chunks[c][0]
        others = recvbuf.at[g, pl.ds(0, owners - 1), :, lanes(c)]
        pltpu.make_async_copy(others, others, rsem.at[c]).wait()
        own = recvbuf.at[g, me, :, lanes(c)]
        pltpu.make_async_copy(own, own, lsem.at[c]).wait()

    def wait_sent(c):
        g = chunks[c][0]
        others = sendbuf.at[g, pl.ds(0, owners - 1), :, lanes(c)]
        pltpu.make_async_copy(others, others, ssem.at[c]).wait()

    for g in range(groups):
        prepare(g)
        if g == 0:
            pl.semaphore_wait(barrier, owners - 1 + times - 1)
        for c in range(len(chunks)):
            if chunks[c][0] == g:
                send(c)

    column = lax.broadcasted_iota(jnp.int32, (npairs, 16 * owners), 1)
    slot = lax.broadcasted_iota(jnp.int32, (npairs, 16 * owners), 0)
    live = slot < count_ref[0]
    for side in range(2):
        ids = jnp.transpose(jnp.broadcast_to(pairs_ref[side : side + 1, :], (LANES, npairs)))
        line = (ids // capacity) * 16 + lax.rem(ids, capacity) * windows
        line = jnp.concatenate([line] * (16 * owners // LANES), axis=1)
        for part in range(2):
            for w in range(windows):
                hit = column == line + (part * 8 + w)
                if side == 0:
                    hit = hit & live
                ohot[side, part, w] = jnp.where(hit, 1.0, 0.0).astype(F32).astype(BF16)

    acc[...] = jnp.zeros(acc.shape, F32)

    def products(g, t0, first):
        at = pl.multiple_of(t0 * LANES, 2 * LANES)
        rows = recvbuf[g, :, :, pl.ds(at, 2 * LANES)].reshape(16 * owners, 2 * LANES)
        real = None
        for w in range(windows):
            a = [jnp.dot(ohot[0, part, w], rows, preferred_element_type=F32) for part in range(2)]
            b = [jnp.dot(ohot[1, part, w], rows, preferred_element_type=F32) for part in range(2)]
            re = a[0] * b[0] + a[1] * b[1]
            im = a[1] * b[0] - a[0] * b[1]
            real, imag = (re, im) if real is None else (real + re, imag + im)
        for i, value in enumerate((real, imag)):
            high = value.astype(BF16)
            low = (value - high.astype(F32)).astype(BF16)
            for t in range(2):
                to = pl.ds(pl.multiple_of((t0 - first + t) * 2 * LANES, 2 * LANES) + i * LANES, LANES)
                dhi[:, to] = high[:, t * LANES : (t + 1) * LANES]
                dlo[:, to] = low[:, t * LANES : (t + 1) * LANES]

    for c, (g, t0, nt) in enumerate(chunks):
        wait_received(c)

        def piece(i, _):
            products(g, t0 + 2 * i, t0)
            return 0

        lax.fori_loop(0, nt // 2, piece, 0)
        if t0 == 0:
            load_table(g).wait()
        depth = nt * 2 * LANES

        def lag_tile(n, _):
            at = pl.ds(pl.multiple_of(n * 256, 256), 256)
            thi = tbuf[g % 2, t0 : t0 + nt, 0, :, at].reshape(depth, 256)
            tlo = tbuf[g % 2, t0 : t0 + nt, 1, :, at].reshape(depth, 256)
            high = dhi[:, :depth]
            total = jnp.dot(high, thi, preferred_element_type=F32)
            total += jnp.dot(dlo[:, :depth], thi, preferred_element_type=F32)
            total += jnp.dot(high, tlo, preferred_element_type=F32)
            acc[:, at] += total
            return 0

        lax.fori_loop(0, LAGS // 256, lag_tile, 0)
        if t0 + nt == GROUP and g + 2 < groups:
            load_table(g + 2).start()

    def give(i, _):
        to = lax.rem(tm + i, times)
        pltpu.make_async_remote_copy(
            src_ref=acc.at[pl.ds(to * share, share), :], dst_ref=summed.at[tm],
            send_sem=psem, recv_sem=qsem, device_id=(me, to), device_id_type=MESH,
        ).start()
        return 0

    lax.fori_loop(1, times, give, 0)
    summed[tm] = acc[pl.ds(pl.multiple_of(tm * share, 8), share), :]
    received = summed.at[pl.ds(0, times - 1)]
    pltpu.make_async_copy(received, received, qsem).wait()
    total = summed[0]
    for t in range(1, times):
        total = total + summed[t]
    out_ref[...] = total * scale
    given = acc.at[pl.ds(0, (times - 1) * share), :]
    pltpu.make_async_copy(given, given, psem).wait()
    for c in range(len(chunks)):
        wait_sent(c)


def shards(table, spectra, send_rows, pair_list, pair_count):
    owners = lax.axis_size("pair")
    times = lax.axis_size("tm")
    channels, windows, _, bins = spectra.shape
    capacity = send_rows.shape[2]
    npairs = pair_list.shape[1]
    tiles = bins // LANES
    groups = tiles // GROUP
    lines = spectra.reshape(channels, windows, 2, tiles, LANES).transpose(0, 1, 3, 2, 4)
    lines = lines.reshape(channels, windows * tiles * 2, LANES)
    chunks = [(g, 0, GROUP) for g in range(groups - 1)]
    chunks += [(groups - 1, 0, 4), (groups - 1, 4, 2), (groups - 1, 6, 2)]
    scale = (2.0 * bins * windows * times) ** (-0.5)
    dims = (owners, times, capacity, windows, groups, npairs, tuple(chunks), scale)
    rows = jnp.transpose(send_rows, (0, 2, 1)).reshape(capacity, owners)
    count = len(chunks)
    dma = pltpu.SemaphoreType.DMA
    return pl.pallas_call(
        functools.partial(kernel, dims),
        out_shape=jax.ShapeDtypeStruct((npairs // times, LAGS), F32),
        in_specs=[
            pl.BlockSpec(memory_space=pl.ANY),
            pl.BlockSpec(memory_space=pltpu.SMEM),
            pl.BlockSpec(memory_space=pltpu.VMEM),
            pl.BlockSpec(memory_space=pltpu.SMEM),
            pl.BlockSpec(memory_space=pl.ANY),
        ],
        out_specs=pl.BlockSpec(memory_space=pltpu.VMEM),
        scratch_shapes=[
            *[pltpu.VMEM((channels, windows * 2 * GROUP, LANES), BF16)] * groups,
            pltpu.VMEM((4 * 16 * GROUP, LANES), F32),
            pltpu.VMEM((groups, owners, 16, GROUP * LANES), BF16),
            pltpu.VMEM((groups, owners, 16, GROUP * LANES), BF16),
            pltpu.VMEM((2, 2, windows, npairs, 16 * owners), BF16),
            pltpu.VMEM((npairs, GROUP * 2 * LANES), BF16),
            pltpu.VMEM((npairs, GROUP * 2 * LANES), BF16),
            pltpu.VMEM((2, GROUP, 2, 2 * LANES, LAGS), BF16),
            pltpu.VMEM((npairs, LAGS), F32),
            pltpu.VMEM((times, npairs // times, LAGS), F32),
            dma((groups, windows)),
            dma((groups,)),
            dma((count,)),
            dma((count,)),
            dma((count,)),
            dma,
            dma,
        ],
        compiler_params=pltpu.CompilerParams(
            collective_id=0, has_side_effects=True, vmem_limit_bytes=56 * 1024 * 1024
        ),
        name="correlate",
    )(lines, rows, pair_list, pair_count, table)


def solution(mesh):
    table = lag_table(4096, LAGS)

    def run(spectra, send_rows, pair_list, pair_count):
        in_specs = (P(), P("pair", "tm", None, None), P("pair", None, None), P(None, "pair"), P("pair"))
        body = jax.shard_map(
            shards, mesh=mesh, in_specs=in_specs, out_specs=P(("pair", "tm"), None), check_vma=False
        )
        return body(jnp.asarray(table), spectra, send_rows, pair_list, pair_count)

    return run
```

time: 672 us -> 130 us (0.19)
  waiting for transfers between devices: 239 us -> 0 us
  matrix products: 149 us -> 0 us
  other arithmetic: 137 us -> 0 us
  Pallas kernels: 0 us -> 127 us
  local copies, waits for them, and re-layouts: 113 us -> 1.62 us
  between operations: 15.2 us -> 0.66 us
  starting transfers between devices: 12.9 us -> 0 us
    dot_general x16 -> x0, matrix products: 149 us -> none  [the longest x8 75.1 us: transform(): total = total - jnp.dot(imag_part, sine, precision=lax.Precision.HIGHEST)]
    unnamed x2 -> x0, waiting for transfers between devices: 148 us -> none
    pallas_call x0 -> x1, Pallas kernels: none -> 127 us  [shards(): pl.pallas_call(functools.partial(kernel, dims), out_shape=jax.ShapeDtypeS...]
    gather x5 -> x0, local copies, waits for them, and re-layouts: 98.2 us -> none  [the longest x2 42.1 us: shards(): jnp.take(arrived_rows[:, window], right_ids, axis=0).astype(jnp.float32)]
    all_to_all x1 -> x0, waiting for transfers between devices: 91.4 us -> none  [shards(): lax.all_to_all(outgoing, 'pair', split_axis=0, concat_axis=0, tiled=True)]
    add x9 -> x0, other arithmetic: 68.5 us -> none  [the longest x2 68.5 us: shards(): left_rows[:, 0] * right_rows[:, 0] + left_rows[:, 1] * right_rows[:, 1]]
    convert_element_type x3 -> x0, other arithmetic: 31.2 us -> none  [the longest x1 17.6 us: shards(): jnp.take(arrived_rows[:, window], left_ids, axis=0).astype(jnp.float32)]
    mul x1 -> x0, other arithmetic: 28.9 us -> none  [shards(): stacked = stacked * active]
  transfers between devices with their start and end apart: 2 -> 0, of which waited for: 2 -> 0; matrix products, arithmetic and copies ran while one was open for 0% -> 0% of each run, Pallas kernels for 0% -> 0%
where the time goes in v1:
time: 130 us
  Pallas kernels  127 us (98%)
  local copies, waits for them, and re-layouts  1.62 us (1%)
    pallas_call x1, Pallas kernels, shards(): pl.pallas_call(functools.partial(kernel, dims), out_shape=jax.ShapeDtypeS...  127 us

profile of v1, /device:TPU:1, one launch (start us, length us, event | category | flops | bytes accessed | tf_op | source)
XLA Modules:
  0.0 129.7 jit_solution(17667311497871002942)
XLA Ops:
  0.7 127.4 %correlate.1 = f32[48,1024]{1,0:T(8,128)} custom-call(bf16[128,128,128]{2,1,0:T(8,128)(2,1)} %bitcast.8, s32[4,32]{1,0:T(4,128)} %bitcast.9, s32[2,384]{1,0:T(2,128)} %pairs_ref.1, s32[1]{0:T(128)S(6)} %copy.8.count_ref, bf16[32,2,256,1024]{3,2,1,0:T(8,128)(2,1)} %constant.2.clone.table_hbm), custom_call_target="tpu_custom_call" | custom-call | tf_op jit(solution)/shard_map/correlate/pallas_call | solution.py:225
  128.1 1.6 %copy.9 = f32[48,1024]{1,0:T(8,128)} copy(f32[48,1024]{1,0:T(8,128)} %correlate.1) | data formatting | bytes 393216

commit v2 on v1

v2 whole, which is shorter than its diff:
```python
import functools
import math

import jax
import jax.numpy as jnp
import numpy as np
from jax import lax
from jax.experimental import pallas as pl
from jax.experimental.pallas import tpu as pltpu
from jax.sharding import PartitionSpec as P

MESH = pl.DeviceIdType.MESH
LAGS = 1024
LANES = 128
GROUP = 8
F32 = jnp.float32
BF16 = jnp.bfloat16


def lag_tables(bins, lags):
    delay = np.arange(lags, dtype=np.int64) - lags // 2

    def pair(freq):
        angle = (freq[:, None] * delay[None, :] % (2 * bins)).astype(np.float64) * (math.pi / bins)
        return np.cos(angle).astype(np.float32), np.sin(angle).astype(np.float32)

    first = np.stack(pair(np.arange(bins // LANES, dtype=np.int64) * LANES), axis=1)
    added = np.stack(pair(np.arange(LANES, dtype=np.int64)))
    return first, added


def kernel(dims, x_hbm, rows_hbm, pairs_hbm, count_hbm, first_hbm, added_hbm, out_ref,
           *scratch):
    owners, times, capacity, windows, groups, npairs, chunks, scale = dims
    xbufs, scratch = scratch[:groups], scratch[groups:]
    rows_ref, pairs_ref, count_ref, stage, sendbuf, latebuf, recvbuf, ohot, scratch = *scratch[:8], scratch[8:]
    dhi, dlo, tbuf, first, added, acc, summed, stack, parts, scratch = *scratch[:9], scratch[9:]
    xsem, tsem, ssem, rsem, lsem, esem, psem, qsem, usem, vsem = scratch
    late = groups - 1
    me = lax.axis_index("pair")
    tm = lax.axis_index("tm")
    share = npairs // times

    def load_x(g, w):
        rows = pl.ds((w * groups + g) * 2 * GROUP, 2 * GROUP)
        to = pl.ds(w * 2 * GROUP, 2 * GROUP)
        return pltpu.make_async_copy(x_hbm.at[:, rows, :], xbufs[g].at[:, to, :], xsem.at[g, w])

    def load_tables():
        return [
            pltpu.make_async_copy(pairs_hbm, pairs_ref, tsem.at[0]),
            pltpu.make_async_copy(count_hbm, count_ref, tsem.at[1]),
            pltpu.make_async_copy(first_hbm, first, tsem.at[2]),
            pltpu.make_async_copy(added_hbm, added, tsem.at[3]),
        ]

    rows_copy = pltpu.make_async_copy(rows_hbm, rows_ref, tsem.at[4])
    rows_copy.start()
    for w in range(windows):
        load_x(0, w).start()

    barrier = pltpu.get_barrier_semaphore()

    def greet_owner(i, _):
        pl.semaphore_signal(barrier, inc=1, device_id=(lax.rem(me + i, owners), tm), device_id_type=MESH)
        return 0

    def greet_time(i, _):
        pl.semaphore_signal(barrier, inc=1, device_id=(me, lax.rem(tm + i, times)), device_id_type=MESH)
        return 0

    lax.fori_loop(1, owners, greet_owner, 0)
    lax.fori_loop(1, times, greet_time, 0)
    for g in range(1, groups):
        for w in range(windows):
            load_x(g, w).start()
    for copy in load_tables():
        copy.start()

    rows_copy.wait()

    def prepare(g):
        for w in range(windows):
            load_x(g, w).wait()

        def one(o, _):
            base = lax.rem(o, 4) * (16 * GROUP)
            for k in range(capacity):
                r = rows_ref[k, o]
                for w in range(windows):
                    v = xbufs[g][r, w * 2 * GROUP : (w + 1) * 2 * GROUP, :]
                    stage[pl.ds(base + k * windows + w, 2 * GROUP, stride=8), :] = v.astype(F32)
            for t in range(GROUP):
                sendbuf[g, o, :, t * LANES : (t + 1) * LANES] = stage[pl.ds(base + t * 16, 16), :].astype(BF16)
            return 0

        lax.fori_loop(0, owners, one, 0, unroll=2)

    def lanes(c):
        g, t0, nt = chunks[c]
        return pl.ds(t0 * LANES, nt * LANES)

    def source(g):
        return latebuf if g == late else sendbuf.at[g]

    def send(c):
        g = chunks[c][0]

        def one(i, _):
            to = lax.rem(me + i, owners)
            pltpu.make_async_remote_copy(
                src_ref=source(g).at[to, :, lanes(c)], dst_ref=recvbuf.at[g, me, :, lanes(c)],
                send_sem=ssem.at[c], recv_sem=rsem.at[c], device_id=(to, tm), device_id_type=MESH,
            ).start()
            return 0

        lax.fori_loop(1, owners, one, 0)
        pltpu.make_async_copy(source(g).at[me, :, lanes(c)], recvbuf.at[g, me, :, lanes(c)], lsem.at[c]).start()

    def wait_received(c):
        g = chunks[c][0]
        others = recvbuf.at[g, pl.ds(0, owners - 1), :, lanes(c)]
        pltpu.make_async_copy(others, others, rsem.at[c]).wait()
        own = recvbuf.at[g, me, :, lanes(c)]
        pltpu.make_async_copy(own, own, lsem.at[c]).wait()

    def wait_sent(c):
        g = chunks[c][0]
        others = source(g).at[pl.ds(0, owners - 1), :, lanes(c)]
        pltpu.make_async_copy(others, others, ssem.at[c]).wait()

    def tile(t):
        return pl.ds(pl.multiple_of(t * LANES, LANES), LANES)

    own_tile = pltpu.make_async_copy(sendbuf.at[late, :, :, tile(tm)], latebuf.at[:, :, tile(tm)], esem.at[2])

    def trade():
        def one(i, _):
            to = lax.rem(tm + i, times)
            pltpu.make_async_remote_copy(
                src_ref=sendbuf.at[late, :, :, tile(to)], dst_ref=latebuf.at[:, :, tile(tm)],
                send_sem=esem.at[0], recv_sem=esem.at[1], device_id=(me, to), device_id_type=MESH,
            ).start()
            return 0

        lax.fori_loop(1, times, one, 0)
        own_tile.start()

    def wait_traded():
        others = latebuf.at[:, :, pl.ds(0, (times - 1) * LANES)]
        pltpu.make_async_copy(others, others, esem.at[1]).wait()
        own_tile.wait()

    for g in (0, late, *range(1, late)):
        prepare(g)
        if g == 0:
            pl.semaphore_wait(barrier, owners - 1 + times - 1)
        if g == late:
            trade()
        for c in range(len(chunks)):
            if chunks[c][0] == g < late:
                send(c)

    for copy in load_tables():
        copy.wait()

    column = lax.broadcasted_iota(jnp.int32, (npairs, 16 * owners), 1)
    slot = lax.broadcasted_iota(jnp.int32, (npairs, 16 * owners), 0)
    live = slot < count_ref[0]
    for side in range(2):
        ids = jnp.transpose(jnp.broadcast_to(pairs_ref[side : side + 1, :], (LANES, npairs)))
        line = (ids // capacity) * 16 + lax.rem(ids, capacity) * windows
        line = jnp.concatenate([line] * (16 * owners // LANES), axis=1)
        for part in range(2):
            for w in range(windows):
                hit = column == line + (part * 8 + w)
                if side == 0:
                    hit = hit & live
                ohot[side, part, w] = jnp.where(hit, 1.0, 0.0).astype(F32).astype(BF16)

    acc[...] = jnp.zeros(acc.shape, F32)

    def split(value):
        high = value.astype(BF16)
        return high, (value - high.astype(F32)).astype(BF16)

    def make_table(g):
        def one(i, _):
            t, n = i // (LAGS // 256), lax.rem(i, LAGS // 256)
            at = pl.ds(pl.multiple_of(n * 256, 256), 256)
            c0, s0 = first[g * GROUP + t, 0:1, at], first[g * GROUP + t, 1:2, at]
            c1, s1 = added[0, :, at], added[1, :, at]
            for row, value in ((0, c0 * c1 - s0 * s1), (LANES, -(s0 * c1 + c0 * s1))):
                high, low = split(value)
                tbuf[t, 0, row : row + LANES, at] = high
                tbuf[t, 1, row : row + LANES, at] = low
            return 0

        lax.fori_loop(0, GROUP * (LAGS // 256), one, 0)

    def cross(g, at, width):
        rows = recvbuf[g, :, :, pl.ds(at, width)].reshape(16 * owners, width)
        real = None
        for w in range(windows):
            a = [jnp.dot(ohot[0, part, w], rows, preferred_element_type=F32) for part in range(2)]
            b = [jnp.dot(ohot[1, part, w], rows, preferred_element_type=F32) for part in range(2)]
            re = a[0] * b[0] + a[1] * b[1]
            im = a[1] * b[0] - a[0] * b[1]
            real, imag = (re, im) if real is None else (real + re, imag + im)
        return real, imag

    def early_chunk(g, t0, nt):
        def piece(i, _):
            at = pl.multiple_of((t0 + 2 * i) * LANES, 2 * LANES)
            for part, value in enumerate(cross(g, at, 2 * LANES)):
                high, low = split(value)
                for t in range(2):
                    to = pl.ds(pl.multiple_of((2 * i + t) * 2 * LANES, 2 * LANES) + part * LANES, LANES)
                    dhi[:, to] = high[:, t * LANES : (t + 1) * LANES]
                    dlo[:, to] = low[:, t * LANES : (t + 1) * LANES]
            return 0

        lax.fori_loop(0, nt // 2, piece, 0)
        depth = nt * 2 * LANES

        def lag_tile(n, _):
            at = pl.ds(pl.multiple_of(n * 256, 256), 256)
            thi = tbuf[t0 : t0 + nt, 0, :, at].reshape(depth, 256)
            tlo = tbuf[t0 : t0 + nt, 1, :, at].reshape(depth, 256)
            high = dhi[:, :depth]
            total = jnp.dot(high, thi, preferred_element_type=F32)
            total += jnp.dot(dlo[:, :depth], thi, preferred_element_type=F32)
            total += jnp.dot(high, tlo, preferred_element_type=F32)
            acc[:, at] += total
            return 0

        lax.fori_loop(0, LAGS // 256, lag_tile, 0)

    def late_chunk(t0, nt):
        def piece(i, _):
            at = pl.multiple_of((t0 + 2 * i) * LANES, 2 * LANES)
            for part, value in enumerate(cross(late, at, 2 * LANES)):
                stack[:, part * LANES : (part + 1) * LANES] += value[:, :LANES] + value[:, LANES:]
            return 0

        if nt > 1:
            lax.fori_loop(0, nt // 2, piece, 0)
        else:
            for part, value in enumerate(cross(late, t0 * LANES, LANES)):
                stack[:, part * LANES : (part + 1) * LANES] += value

    def block(t):
        return pl.ds(pl.multiple_of(t * share, 8), share)

    def give(src, dst, send_sem, recv_sem):
        def one(i, _):
            to = lax.rem(tm + i, times)
            pltpu.make_async_remote_copy(
                src_ref=src.at[block(to), :], dst_ref=dst.at[tm], send_sem=send_sem, recv_sem=recv_sem.at[i],
                device_id=(me, to), device_id_type=MESH,
            ).start()
            return 0

        lax.fori_loop(1, times, one, 0)

    def wait_given(src, sem):
        given = src.at[pl.ds(0, (times - 1) * share), :]
        pltpu.make_async_copy(given, given, sem).wait()

    def wait_part(dst, sem, i):
        come = dst.at[lax.rem(tm + times - i, times)]
        pltpu.make_async_copy(come, come, sem.at[i]).wait()

    stack[...] = jnp.zeros(stack.shape, F32)
    for c, (g, t0, nt) in enumerate(chunks):
        if t0 == 0:
            make_table(g)
        if c == 1:
            wait_traded()
            for d in range(len(chunks)):
                if chunks[d][0] == late:
                    send(d)
        wait_received(c)
        if g < late:
            early_chunk(g, t0, nt)
        else:
            late_chunk(t0, nt)
        if g < late and chunks[c + 1][0] == late:
            give(acc, summed, psem, qsem)

    give(stack, parts, usem, vsem)
    for i in range(1, times):
        wait_part(summed, qsem, i)
    summed[tm] = acc[block(tm), :]
    total = summed[0]
    for t in range(1, times):
        total = total + summed[t]
    out_ref[...] = total * scale
    parts[tm] = stack[block(tm), :]

    def lag_part(j, _):
        odd = lax.rem(j, 2)
        i = odd * ((j + 1) // 2) + (1 - odd) * (lax.rem(times - j // 2, times))

        @pl.when(j > 0)
        def _():
            wait_part(parts, vsem, i)

        t = lax.rem(tm + times - i, times)
        high, low = split(parts[t])
        thi, tlo = tbuf[t, 0], tbuf[t, 1]
        value = jnp.dot(jnp.concatenate([high, low]), thi, preferred_element_type=F32)
        value = value[:share] + value[share:] + jnp.dot(high, tlo, preferred_element_type=F32)
        out_ref[...] += value * scale
        return 0

    lax.fori_loop(0, times, lag_part, 0)
    wait_given(acc, psem)
    wait_given(stack, usem)
    others = sendbuf.at[late, :, :, pl.ds(0, (times - 1) * LANES)]
    pltpu.make_async_copy(others, others, esem.at[0]).wait()
    for c in range(len(chunks)):
        wait_sent(c)


def shards(first, added, spectra, send_rows, pair_list, pair_count):
    owners = lax.axis_size("pair")
    times = lax.axis_size("tm")
    channels, windows, _, bins = spectra.shape
    capacity = send_rows.shape[2]
    npairs = pair_list.shape[1]
    tiles = bins // LANES
    groups = tiles // GROUP
    lines = spectra.reshape(channels, windows, 2, tiles, LANES).transpose(0, 1, 3, 2, 4)
    lines = lines.reshape(channels, windows * tiles * 2, LANES)
    last = groups - 1
    chunks = [(g, 0, GROUP) for g in range(last - 1)]
    chunks += [(last - 1, 0, 4), (last - 1, 4, 2), (last - 1, 6, 2)]
    chunks += [(last, 0, 4), (last, 4, 2), (last, 6, 1), (last, 7, 1)]
    scale = (2.0 * bins * windows * times) ** (-0.5)
    dims = (owners, times, capacity, windows, groups, npairs, tuple(chunks), scale)
    rows = jnp.transpose(send_rows, (0, 2, 1)).reshape(capacity, owners)
    nc = len(chunks)
    dma = pltpu.SemaphoreType.DMA
    return pl.pallas_call(
        functools.partial(kernel, dims),
        out_shape=pltpu.VMEM((npairs // times, LAGS), F32),
        in_specs=[pl.BlockSpec(memory_space=pltpu.HBM)] * 6,
        out_specs=pl.BlockSpec(memory_space=pltpu.VMEM),
        scratch_shapes=[
            *[pltpu.VMEM((channels, windows * 2 * GROUP, LANES), BF16)] * groups,
            pltpu.SMEM(rows.shape, jnp.int32),
            pltpu.VMEM(pair_list.shape, jnp.int32),
            pltpu.SMEM((1,), jnp.int32),
            pltpu.VMEM((4 * 16 * GROUP, LANES), F32),
            pltpu.VMEM((groups, owners, 16, GROUP * LANES), BF16),
            pltpu.VMEM((owners, 16, GROUP * LANES), BF16),
            pltpu.VMEM((groups, owners, 16, GROUP * LANES), BF16),
            pltpu.VMEM((2, 2, windows, npairs, 16 * owners), BF16),
            pltpu.VMEM((npairs, GROUP * 2 * LANES), BF16),
            pltpu.VMEM((npairs, GROUP * 2 * LANES), BF16),
            pltpu.VMEM((GROUP, 2, 2 * LANES, LAGS), BF16),
            pltpu.VMEM(first.shape, F32),
            pltpu.VMEM(added.shape, F32),
            pltpu.VMEM((npairs, LAGS), F32),
            pltpu.VMEM((times, npairs // times, LAGS), F32),
            pltpu.VMEM((npairs, 2 * LANES), F32),
            pltpu.VMEM((times, npairs // times, 2 * LANES), F32),
            dma((groups, windows)),
            dma((5,)),
            dma((nc,)),
            dma((nc,)),
            dma((nc,)),
            dma((3,)),
            dma,
            dma((times,)),
            dma,
            dma((times,)),
        ],
        compiler_params=pltpu.CompilerParams(
            collective_id=0, has_side_effects=True, vmem_limit_bytes=58 * 1024 * 1024
        ),
        name="correlate",
    )(lines, rows, pair_list, pair_count, first, added)


def solution(mesh):
    first, added = lag_tables(4096, LAGS)

    def run(spectra, send_rows, pair_list, pair_count):
        in_specs = (P(), P(), P("pair", "tm", None, None), P("pair", None, None), P(None, "pair"), P("pair"))
        body = jax.shard_map(
            shards, mesh=mesh, in_specs=in_specs, out_specs=P(("pair", "tm"), None), check_vma=False
        )
        return body(jnp.asarray(first), jnp.asarray(added), spectra, send_rows, pair_list, pair_count)

    return run
```

time: 130 us -> 114 us (0.88)
  Pallas kernels: 127 us -> 112 us
    pallas_call x1, Pallas kernels: 127 us -> 112 us  [shards(): pl.pallas_call(functools.partial(kernel, dims), out_shape=pltpu.VMEM((npa...]
where the time goes in v2:
time: 114 us
  Pallas kernels  112 us (98%)
    pallas_call x1, Pallas kernels, shards(): pl.pallas_call(functools.partial(kernel, dims), out_shape=pltpu.VMEM((npa...  112 us

profile of v2, /device:TPU:1, one launch (start us, length us, event | category | flops | bytes accessed | tf_op | source)
XLA Modules:
  0.0 113.8 jit_solution(12076620989914875548)
XLA Ops:
  0.7 112.4 %correlate.1 = f32[48,1024]{1,0:T(8,128)S(1)} custom-call(bf16[128,128,128]{2,1,0:T(8,128)(2,1)} %bitcast.8, s32[4,32]{1,0:T(4,128)} %bitcast.9, s32[2,384]{1,0:T(2,128)} %pairs_hbm.1, s32[1]{0:T(128)S(6)} %copy.10.count_hbm, f32[32,2,1024]{2,1,0:T(2,128)} %constant.4.clone.first_hbm, f32[2,128,1024]{2,1,0:T(8,128)} %constant.5.clone.added_hbm), custom_call_target="tpu_custom_call" | custom-call | tf_op jit(solution)/shard_map/correlate/pallas_call | solution.py:345
  113.1 0.7 copy.9

commit v3 on v2

--- a/solution.py
+++ b/solution.py
@@ -12,6 +12,7 @@
 MESH = pl.DeviceIdType.MESH
 LAGS = 1024
 LANES = 128
+HALF = LANES // 2
 GROUP = 8
 F32 = jnp.float32
 BF16 = jnp.bfloat16
@@ -34,7 +35,7 @@
     owners, times, capacity, windows, groups, npairs, chunks, scale = dims
     xbufs, scratch = scratch[:groups], scratch[groups:]
     rows_ref, pairs_ref, count_ref, stage, sendbuf, latebuf, recvbuf, ohot, scratch = *scratch[:8], scratch[8:]
-    dhi, dlo, tbuf, first, added, acc, summed, stack, parts, scratch = *scratch[:9], scratch[9:]
+    dhi, dlo, tbuf, first, added, acc, summed, sums, stack, parts, packed, scratch = *scratch[:11], scratch[11:]
     xsem, tsem, ssem, rsem, lsem, esem, psem, qsem, usem, vsem = scratch
     late = groups - 1
     me = lax.axis_index("pair")
@@ -151,6 +152,19 @@
         pltpu.make_async_copy(others, others, esem.at[1]).wait()
         own_tile.wait()
 
+        def pack(o, _):
+            for row in range(times // 2):
+                x = latebuf[o, :, row * 2 * LANES : (row * 2 + 1) * LANES].astype(F32)
+                y = latebuf[o, :, (row * 2 + 1) * LANES : (row * 2 + 2) * LANES].astype(F32)
+                for h in range(2):
+                    cut = slice(h * HALF, (h + 1) * HALF)
+                    packed[h * (times // 2) + row] = jnp.concatenate([x[:, cut], y[:, cut]], axis=1).astype(BF16)
+            for t in range(times):
+                latebuf[o, :, t * LANES : (t + 1) * LANES] = packed[t]
+            return 0
+
+        lax.fori_loop(0, owners, pack, 0)
+
     for g in (0, late, *range(1, late)):
         prepare(g)
         if g == 0:
@@ -164,19 +178,18 @@
     for copy in load_tables():
         copy.wait()
 
-    column = lax.broadcasted_iota(jnp.int32, (npairs, 16 * owners), 1)
-    slot = lax.broadcasted_iota(jnp.int32, (npairs, 16 * owners), 0)
+    lines = 8 * owners
+    column = lax.broadcasted_iota(jnp.int32, (npairs, lines), 1)
+    slot = lax.broadcasted_iota(jnp.int32, (npairs, lines), 0)
     live = slot < count_ref[0]
     for side in range(2):
         ids = jnp.transpose(jnp.broadcast_to(pairs_ref[side : side + 1, :], (LANES, npairs)))
-        line = (ids // capacity) * 16 + lax.rem(ids, capacity) * windows
-        line = jnp.concatenate([line] * (16 * owners // LANES), axis=1)
-        for part in range(2):
-            for w in range(windows):
-                hit = column == line + (part * 8 + w)
-                if side == 0:
-                    hit = hit & live
-                ohot[side, part, w] = jnp.where(hit, 1.0, 0.0).astype(F32).astype(BF16)
+        line = jnp.concatenate([ids * windows] * (lines // LANES), axis=1)
+        for w in range(windows):
+            hit = column == line + w
+            if side == 0:
+                hit = hit & live
+            ohot[side, w] = jnp.where(hit, 1.0, 0.0).astype(F32).astype(BF16)
 
     acc[...] = jnp.zeros(acc.shape, F32)
 
@@ -190,20 +203,27 @@
             at = pl.ds(pl.multiple_of(n * 256, 256), 256)
             c0, s0 = first[g * GROUP + t, 0:1, at], first[g * GROUP + t, 1:2, at]
             c1, s1 = added[0, :, at], added[1, :, at]
-            for row, value in ((0, c0 * c1 - s0 * s1), (LANES, -(s0 * c1 + c0 * s1))):
-                high, low = split(value)
-                tbuf[t, 0, row : row + LANES, at] = high
-                tbuf[t, 1, row : row + LANES, at] = low
+            for part, value in enumerate((c0 * c1 - s0 * s1, -(s0 * c1 + c0 * s1))):
+                for i, piece in enumerate(split(value)):
+                    if g == late:
+                        for h in range(2):
+                            row = h * LANES + part * HALF
+                            tbuf[t, i, row : row + HALF, at] = piece[h * HALF : (h + 1) * HALF]
+                    else:
+                        tbuf[t, i, part * LANES : (part + 1) * LANES, at] = piece
             return 0
 
         lax.fori_loop(0, GROUP * (LAGS // 256), one, 0)
 
     def cross(g, at, width):
-        rows = recvbuf[g, :, :, pl.ds(at, width)].reshape(16 * owners, width)
+        both = recvbuf[g, :, :, pl.ds(at, width)].astype(F32)
+        rows = [both[:, part * 8 : part * 8 + 8, :].reshape(8 * owners, width).astype(BF16) for part in range(2)]
+        rows = jnp.concatenate(rows, axis=1)
         real = None
         for w in range(windows):
-            a = [jnp.dot(ohot[0, part, w], rows, preferred_element_type=F32) for part in range(2)]
-            b = [jnp.dot(ohot[1, part, w], rows, preferred_element_type=F32) for part in range(2)]
+            a = jnp.dot(ohot[0, w], rows, preferred_element_type=F32)
+            b = jnp.dot(ohot[1, w], rows, preferred_element_type=F32)
+            a, b = [(v[:, :width], v[:, width:]) for v in (a, b)]
             re = a[0] * b[0] + a[1] * b[1]
             im = a[1] * b[0] - a[0] * b[1]
             real, imag = (re, im) if real is None else (real + re, imag + im)
@@ -240,23 +260,32 @@
         def piece(i, _):
             at = pl.multiple_of((t0 + 2 * i) * LANES, 2 * LANES)
             for part, value in enumerate(cross(late, at, 2 * LANES)):
-                stack[:, part * LANES : (part + 1) * LANES] += value[:, :LANES] + value[:, LANES:]
-            return 0
-
+                sums[part] += value[:, :LANES] + value[:, LANES:]
+            return 0
+
+        if t0 % (times // 2) == 0:
+            sums[...] = jnp.zeros(sums.shape, F32)
         if nt > 1:
             lax.fori_loop(0, nt // 2, piece, 0)
         else:
             for part, value in enumerate(cross(late, t0 * LANES, LANES)):
-                stack[:, part * LANES : (part + 1) * LANES] += value
+                sums[part] += value
+
+    def finish_half(h):
+        halves = [sums[part, :, :HALF] + sums[part, :, HALF:] for part in range(2)]
+        stack[h] = jnp.concatenate(halves, axis=1)
+        give(stack.at[h], parts.at[h], usem.at[h], vsem.at[h])
+        parts[h, tm] = stack[h, block(tm), :]
 
     def block(t):
         return pl.ds(pl.multiple_of(t * share, 8), share)
 
     def give(src, dst, send_sem, recv_sem):
         def one(i, _):
-            to = lax.rem(tm + i, times)
+            far = lax.rem(i, 2) * (times // 2 + (i - 1) // 2) + (1 - lax.rem(i, 2)) * (times // 2 - i // 2)
+            to = lax.rem(tm + far, times)
             pltpu.make_async_remote_copy(
-                src_ref=src.at[block(to), :], dst_ref=dst.at[tm], send_sem=send_sem, recv_sem=recv_sem.at[i],
+                src_ref=src.at[block(to), :], dst_ref=dst.at[tm], send_sem=send_sem, recv_sem=recv_sem.at[far],
                 device_id=(me, to), device_id_type=MESH,
             ).start()
             return 0
@@ -271,7 +300,6 @@
         come = dst.at[lax.rem(tm + times - i, times)]
         pltpu.make_async_copy(come, come, sem.at[i]).wait()
 
-    stack[...] = jnp.zeros(stack.shape, F32)
     for c, (g, t0, nt) in enumerate(chunks):
         if t0 == 0:
             make_table(g)
@@ -283,40 +311,55 @@
         wait_received(c)
         if g < late:
             early_chunk(g, t0, nt)
+            if chunks[c + 1][0] == late:
+                give(acc, summed, psem, qsem)
         else:
             late_chunk(t0, nt)
-        if g < late and chunks[c + 1][0] == late:
-            give(acc, summed, psem, qsem)
-
-    give(stack, parts, usem, vsem)
+            if (t0 + nt) % (times // 2) == 0:
+                finish_half(t0 // (times // 2))
+
     for i in range(1, times):
         wait_part(summed, qsem, i)
     summed[tm] = acc[block(tm), :]
     total = summed[0]
     for t in range(1, times):
         total = total + summed[t]
-    out_ref[...] = total * scale
-    parts[tm] = stack[block(tm), :]
-
-    def lag_part(j, _):
+    out_ref[...] = total
+
+    def shift(j):
         odd = lax.rem(j, 2)
-        i = odd * ((j + 1) // 2) + (1 - odd) * (lax.rem(times - j // 2, times))
-
-        @pl.when(j > 0)
-        def _():
-            wait_part(parts, vsem, i)
-
-        t = lax.rem(tm + times - i, times)
-        high, low = split(parts[t])
-        thi, tlo = tbuf[t, 0], tbuf[t, 1]
-        value = jnp.dot(jnp.concatenate([high, low]), thi, preferred_element_type=F32)
-        value = value[:share] + value[share:] + jnp.dot(high, tlo, preferred_element_type=F32)
-        out_ref[...] += value * scale
-        return 0
-
-    lax.fori_loop(0, times, lag_part, 0)
+        return odd * ((j + 1) // 2) + (1 - odd) * lax.rem(times - j // 2, times)
+
+    for h in range(2):
+
+        def lag_part(step, _):
+            high, low, thi, tlo = [], [], [], []
+            for side in range(2):
+                i = shift(2 * step + side)
+                if side:
+                    wait_part(parts.at[h], vsem.at[h], i)
+                else:
+
+                    @pl.when(step > 0)
+                    def _():
+                        wait_part(parts.at[h], vsem.at[h], i)
+
+                t = lax.rem(tm + times - i, times)
+                for part, into in zip(split(parts[h, t]), (high, low)):
+                    into.append(part)
+                thi.append(tbuf[t, 0, h * LANES : (h + 1) * LANES])
+                tlo.append(tbuf[t, 1, h * LANES : (h + 1) * LANES])
+            high, low = jnp.concatenate(high, axis=1), jnp.concatenate(low, axis=1)
+            value = jnp.dot(jnp.concatenate([high, low]), jnp.concatenate(thi), preferred_element_type=F32)
+            value = value[:share] + value[share:] + jnp.dot(high, jnp.concatenate(tlo), preferred_element_type=F32)
+            out_ref[...] += value
+            return 0
+
+        lax.fori_loop(0, times // 2, lag_part, 0)
+    out_ref[...] *= scale
     wait_given(acc, psem)
-    wait_given(stack, usem)
+    for h in range(2):
+        wait_given(stack.at[h], usem.at[h])
     others = sendbuf.at[late, :, :, pl.ds(0, (times - 1) * LANES)]
     pltpu.make_async_copy(others, others, esem.at[0]).wait()
     for c in range(len(chunks)):
@@ -356,7 +399,7 @@
             pltpu.VMEM((groups, owners, 16, GROUP * LANES), BF16),
             pltpu.VMEM((owners, 16, GROUP * LANES), BF16),
             pltpu.VMEM((groups, owners, 16, GROUP * LANES), BF16),
-            pltpu.VMEM((2, 2, windows, npairs, 16 * owners), BF16),
+            pltpu.VMEM((2, windows, npairs, 8 * owners), BF16),
             pltpu.VMEM((npairs, GROUP * 2 * LANES), BF16),
             pltpu.VMEM((npairs, GROUP * 2 * LANES), BF16),
             pltpu.VMEM((GROUP, 2, 2 * LANES, LAGS), BF16),
@@ -364,8 +407,10 @@
             pltpu.VMEM(added.shape, F32),
             pltpu.VMEM((npairs, LAGS), F32),
             pltpu.VMEM((times, npairs // times, LAGS), F32),
-            pltpu.VMEM((npairs, 2 * LANES), F32),
-            pltpu.VMEM((times, npairs // times, 2 * LANES), F32),
+            pltpu.VMEM((2, npairs, LANES), F32),
+            pltpu.VMEM((2, npairs, LANES), F32),
+            pltpu.VMEM((2, times, npairs // times, LANES), F32),
+            pltpu.VMEM((times, 16, LANES), BF16),
             dma((groups, windows)),
             dma((5,)),
             dma((nc,)),
@@ -374,8 +419,8 @@
             dma((3,)),
             dma,
             dma((times,)),
-            dma,
-            dma((times,)),
+            dma((2,)),
+            dma((2, times)),
         ],
         compiler_params=pltpu.CompilerParams(
             collective_id=0, has_side_effects=True, vmem_limit_bytes=58 * 1024 * 1024

time: 114 us -> 111 us (0.974)
  Pallas kernels: 112 us -> 110 us
    pallas_call x1, Pallas kernels: 112 us -> 110 us  [shards(): pl.pallas_call(functools.partial(kernel, dims), out_shape=pltpu.VMEM((npa...]
where the time goes in v3:
time: 111 us
  Pallas kernels  110 us (99%)
    pallas_call x1, Pallas kernels, shards(): pl.pallas_call(functools.partial(kernel, dims), out_shape=pltpu.VMEM((npa...  110 us

profile of v3, /device:TPU:1, one launch (start us, length us, event | category | flops | bytes accessed | tf_op | source)
XLA Modules:
  0.0 111.3 jit_solution(16100401393442595339)
XLA Ops:
  0.7 109.9 %correlate.1 = f32[48,1024]{1,0:T(8,128)S(1)} custom-call(bf16[128,128,128]{2,1,0:T(8,128)(2,1)} %bitcast.8, s32[4,32]{1,0:T(4,128)} %bitcast.9, s32[2,384]{1,0:T(2,128)} %pairs_hbm.1, s32[1]{0:T(128)S(6)} %copy.10.count_hbm, f32[32,2,1024]{2,1,0:T(2,128)} %constant.4.clone.first_hbm, f32[2,128,1024]{2,1,0:T(8,128)} %constant.5.clone.added_hbm), custom_call_target="tpu_custom_call" | custom-call | tf_op jit(solution)/shard_map/correlate/pallas_call | solution.py:388
  110.6 0.7 copy.9

commit v4 on v3

--- a/solution.py
+++ b/solution.py
@@ -36,7 +36,7 @@
     xbufs, scratch = scratch[:groups], scratch[groups:]
     rows_ref, pairs_ref, count_ref, stage, sendbuf, latebuf, recvbuf, ohot, scratch = *scratch[:8], scratch[8:]
     dhi, dlo, tbuf, first, added, acc, summed, sums, stack, parts, packed, scratch = *scratch[:11], scratch[11:]
-    xsem, tsem, ssem, rsem, lsem, esem, psem, qsem, usem, vsem = scratch
+    xsem, tsem, ssem, rsem, lsem, esem, psem, qsem, usem, vsem, rowsem = scratch
     late = groups - 1
     me = lax.axis_index("pair")
     tm = lax.axis_index("tm")
@@ -62,15 +62,29 @@
 
     barrier = pltpu.get_barrier_semaphore()
 
+    deep = 8
+    wide = owners // deep
+    y, z = me // deep, lax.rem(me, deep)
+
+    def owner_at(dy, dz):
+        return lax.rem(y + dy, wide) * deep + lax.rem(z + dz, deep)
+
+    def near(i):
+        along_y = i // deep
+        return owner_at(along_y * lax.rem(i + 1, deep), (1 - along_y) * lax.rem(i, deep))
+
+    def far(i):
+        return owner_at(1 + i // (deep - 1), 1 + lax.rem(i, deep - 1))
+
     def greet_owner(i, _):
-        pl.semaphore_signal(barrier, inc=1, device_id=(lax.rem(me + i, owners), tm), device_id_type=MESH)
+        pl.semaphore_signal(barrier, inc=1, device_id=(near(i), tm), device_id_type=MESH)
         return 0
 
     def greet_time(i, _):
         pl.semaphore_signal(barrier, inc=1, device_id=(me, lax.rem(tm + i, times)), device_id_type=MESH)
         return 0
 
-    lax.fori_loop(1, owners, greet_owner, 0)
+    lax.fori_loop(1, deep + wide - 1, greet_owner, 0)
     lax.fori_loop(1, times, greet_time, 0)
     for g in range(1, groups):
         for w in range(windows):
@@ -107,15 +121,30 @@
     def send(c):
         g = chunks[c][0]
 
-        def one(i, _):
-            to = lax.rem(me + i, owners)
+        def start(to):
             pltpu.make_async_remote_copy(
                 src_ref=source(g).at[to, :, lanes(c)], dst_ref=recvbuf.at[g, me, :, lanes(c)],
                 send_sem=ssem.at[c], recv_sem=rsem.at[c], device_id=(to, tm), device_id_type=MESH,
             ).start()
-            return 0
-
-        lax.fori_loop(1, owners, one, 0)
+
+        def one_near(i, _):
+            start(near(i))
+            return 0
+
+        def one_far(i, _):
+            start(far(i))
+            return 0
+
+        def pass_on(i, _):
+            pl.semaphore_signal(rowsem, inc=1, device_id=(owner_at(i, 0), tm), device_id_type=MESH)
+            return 0
+
+        if c == 0:
+            lax.fori_loop(1, wide, pass_on, 0)
+        lax.fori_loop(1, deep + wide - 1, one_near, 0)
+        if c == 0:
+            pl.semaphore_wait(rowsem, wide - 1)
+        lax.fori_loop(0, (deep - 1) * (wide - 1), one_far, 0)
         pltpu.make_async_copy(source(g).at[me, :, lanes(c)], recvbuf.at[g, me, :, lanes(c)], lsem.at[c]).start()
 
     def wait_received(c):
@@ -168,7 +197,7 @@
     for g in (0, late, *range(1, late)):
         prepare(g)
         if g == 0:
-            pl.semaphore_wait(barrier, owners - 1 + times - 1)
+            pl.semaphore_wait(barrier, deep + wide - 2 + times - 1)
         if g == late:
             trade()
         for c in range(len(chunks)):
@@ -378,8 +407,8 @@
     lines = lines.reshape(channels, windows * tiles * 2, LANES)
     last = groups - 1
     chunks = [(g, 0, GROUP) for g in range(last - 1)]
-    chunks += [(last - 1, 0, 4), (last - 1, 4, 2), (last - 1, 6, 2)]
-    chunks += [(last, 0, 4), (last, 4, 2), (last, 6, 1), (last, 7, 1)]
+    chunks += [(last - 1, a, b) for a, b in [(0, 4), (4, 4)]]
+    chunks += [(last, a, b) for a, b in [(0, 4), (4, 2), (6, 2)]]
     scale = (2.0 * bins * windows * times) ** (-0.5)
     dims = (owners, times, capacity, windows, groups, npairs, tuple(chunks), scale)
     rows = jnp.transpose(send_rows, (0, 2, 1)).reshape(capacity, owners)
@@ -421,6 +450,7 @@
             dma((times,)),
             dma((2,)),
             dma((2, times)),
+            pltpu.SemaphoreType.REGULAR,
         ],
         compiler_params=pltpu.CompilerParams(
             collective_id=0, has_side_effects=True, vmem_limit_bytes=58 * 1024 * 1024

time: 111 us -> 111 us (level)
  no operation moved by 1% of the time
where the time goes in v4:
time: 111 us
  Pallas kernels  109 us (98%)
    pallas_call x1, Pallas kernels, shards(): pl.pallas_call(functools.partial(kernel, dims), out_shape=pltpu.VMEM((npa...  109 us

profile of v4, /device:TPU:1, one launch (start us, length us, event | category | flops | bytes accessed | tf_op | source)
XLA Modules:
  0.0 110.5 jit_solution(6274070303078155078)
XLA Ops:
  0.7 109.2 %correlate.1 = f32[48,1024]{1,0:T(8,128)S(1)} custom-call(bf16[128,128,128]{2,1,0:T(8,128)(2,1)} %bitcast.8, s32[4,32]{1,0:T(4,128)} %bitcast.9, s32[2,384]{1,0:T(2,128)} %pairs_hbm.1, s32[1]{0:T(128)S(6)} %copy.10.count_hbm, f32[32,2,1024]{2,1,0:T(2,128)} %constant.4.clone.first_hbm, f32[2,128,1024]{2,1,0:T(8,128)} %constant.5.clone.added_hbm), custom_call_target="tpu_custom_call" | custom-call | tf_op jit(solution)/shard_map/correlate/pallas_call | solution.py:417
  109.8 0.7 copy.9

commit v5 on v4

--- a/solution.py
+++ b/solution.py
@@ -141,10 +141,11 @@
 
         if c == 0:
             lax.fori_loop(1, wide, pass_on, 0)
-        lax.fori_loop(1, deep + wide - 1, one_near, 0)
-        if c == 0:
+            lax.fori_loop(1, deep + wide - 1, one_near, 0)
             pl.semaphore_wait(rowsem, wide - 1)
         lax.fori_loop(0, (deep - 1) * (wide - 1), one_far, 0)
+        if c:
+            lax.fori_loop(1, deep + wide - 1, one_near, 0)
         pltpu.make_async_copy(source(g).at[me, :, lanes(c)], recvbuf.at[g, me, :, lanes(c)], lsem.at[c]).start()
 
     def wait_received(c):

time: 111 us -> 110 us (level)
  no operation moved by 1% of the time
where the time goes in v5:
time: 110 us
  Pallas kernels  108 us (98%)
    pallas_call x1, Pallas kernels, shards(): pl.pallas_call(functools.partial(kernel, dims), out_shape=pltpu.VMEM((npa...  108 us

profile of v5, /device:TPU:1, one launch (start us, length us, event | category | flops | bytes accessed | tf_op | source)
XLA Modules:
  0.0 109.7 jit_solution(13094323327218996886)
XLA Ops:
  0.7 108.3 %correlate.1 = f32[48,1024]{1,0:T(8,128)S(1)} custom-call(bf16[128,128,128]{2,1,0:T(8,128)(2,1)} %bitcast.8, s32[4,32]{1,0:T(4,128)} %bitcast.9, s32[2,384]{1,0:T(2,128)} %pairs_hbm.1, s32[1]{0:T(128)S(6)} %copy.10.count_hbm, f32[32,2,1024]{2,1,0:T(2,128)} %constant.4.clone.first_hbm, f32[2,128,1024]{2,1,0:T(8,128)} %constant.5.clone.added_hbm), custom_call_target="tpu_custom_call" | custom-call | tf_op jit(solution)/shard_map/correlate/pallas_call | solution.py:418
  109.0 0.7 copy.9

commit v6 on v5

--- a/solution.py
+++ b/solution.py
@@ -71,7 +71,9 @@
 
     def near(i):
         along_y = i // deep
-        return owner_at(along_y * lax.rem(i + 1, deep), (1 - along_y) * lax.rem(i, deep))
+        odd = lax.rem(i, 2)
+        dz = odd * ((i + 1) // 2) + (1 - odd) * (deep - i // 2)
+        return owner_at(along_y * lax.rem(i + 1, deep), (1 - along_y) * dz)
 
     def far(i):
         return owner_at(1 + i // (deep - 1), 1 + lax.rem(i, deep - 1))
@@ -145,7 +147,7 @@
             pl.semaphore_wait(rowsem, wide - 1)
         lax.fori_loop(0, (deep - 1) * (wide - 1), one_far, 0)
         if c:
-            lax.fori_loop(1, deep + wide - 1, one_near, 0)
+            lax.fori_loop(1, deep + wide - 1, lambda i, _: one_near(deep + wide - 1 - i, 0), 0)
         pltpu.make_async_copy(source(g).at[me, :, lanes(c)], recvbuf.at[g, me, :, lanes(c)], lsem.at[c]).start()
 
     def wait_received(c):

time: 110 us -> 110 us (level)
  no operation moved by 1% of the time
where the time goes in v6:
time: 110 us
  Pallas kernels  109 us (99%)
    pallas_call x1, Pallas kernels, shards(): pl.pallas_call(functools.partial(kernel, dims), out_shape=pltpu.VMEM((npa...  109 us

profile of v6, /device:TPU:1, one launch (start us, length us, event | category | flops | bytes accessed | tf_op | source)
XLA Modules:
  0.0 109.9 jit_solution(12111928616928018690)
XLA Ops:
  0.7 108.6 %correlate.1 = f32[48,1024]{1,0:T(8,128)S(1)} custom-call(bf16[128,128,128]{2,1,0:T(8,128)(2,1)} %bitcast.8, s32[4,32]{1,0:T(4,128)} %bitcast.9, s32[2,384]{1,0:T(2,128)} %pairs_hbm.1, s32[1]{0:T(128)S(6)} %copy.10.count_hbm, f32[32,2,1024]{2,1,0:T(2,128)} %constant.4.clone.first_hbm, f32[2,128,1024]{2,1,0:T(8,128)} %constant.5.clone.added_hbm), custom_call_target="tpu_custom_call" | custom-call | tf_op jit(solution)/shard_map/correlate/pallas_call | solution.py:420
  109.2 0.7 copy.9
